TPU v7x, 256 devices: a whole 4x4x8 slice. The times are simulated.
256 devices in a mesh: section: 16 (over x, y_hi, core), seq: 16 (over z, y_lo).
Axes of the slice: x: 4, y: 4 (y_hi: 2, y_lo: 2; y = y_hi * 2 + y_lo), z: 8, core: 2. Of those that a mesh axis runs over, the one named last changes fastest.
Arguments:
- grad_out: bfloat16 [16, 2048, 2048], P('section', 'seq'), may hold values from -6 to 6
- block_input: bfloat16 [16, 2048, 2048], P('section', 'seq'), may hold values from -5 to 5
- skip_saved: bfloat16 [16, 2048, 2048], P('section', 'seq'), may hold values from -2 to 2
- saved_qkv: bfloat16 [16, 3, 2048, 2048], P('section', None, None, 'seq'), may hold values from -16 to 16
- out_weight: bfloat16 [16, 2048, 2048], P('section', 'seq'), may hold values from -0.125 to 0.125
- qkv_weight: bfloat16 [16, 3, 2048, 2048], P('section', None, 'seq'), may hold values from -0.125 to 0.125
- gate: float32 [16, 2048], P('section'), may hold values from 0.5 to 1.5
- norm_scale: float32 [16, 2048], P('section'), may hold values from -0.5 to 0.5
- skip_gain: float32 [16, 2048], P('section'), may hold values from 0.3 to 1.5
Outputs:
- next_grad: bfloat16 [16, 2048, 2048], P('section', 'seq')
- down_grad: bfloat16 [16, 2048, 2048], P('section', 'seq')
- gain_grad: float32 [16, 2048], P('section')
All inputs are finite; a program needn't handle non-finite values.
Results may differ from a plain program's by a relative error of at most 0.015.
Values may be sent and summed in bfloat16 or wider, within the bound.
A program may use at most 128 MiB of HBM per device.

v0:
```python
import jax
import jax.numpy as jnp
from jax import lax
from jax.sharding import Mesh
from jax.sharding import PartitionSpec as P

HEAD_DIM = 128
SEQ = ("seq_0", "seq_1")


norm_eps = 1e-06


def sum_by_axis(terms, axes):
    running = terms.astype(jnp.bfloat16)
    for axis in axes:
        running = lax.psum_scatter(running, axis, scatter_dimension=0, tiled=True)
    return running.astype(jnp.float32)


def passed_along(block, axis, distance):
    devices = range(lax.axis_size(axis))
    route = [(i - distance, i) for i in devices if i - distance in devices]
    return lax.ppermute(block, axis, route)


def copy_for_each(x, axis):
    copies = jnp.broadcast_to(x, (lax.axis_size(axis), *x.shape))
    return lax.all_to_all(copies, axis, split_axis=0, concat_axis=0, tiled=True)


def taken_together(x, axis):
    return copy_for_each(x, axis).sum(axis=0)


def local_attention(query_all, keys_all, values_all, grad_cols, head_size):
    factor = head_size ** (-0.5)
    total_rows = query_all.shape[0]
    block_rows = min(512, total_rows)
    block_count = total_rows // block_rows
    query_out, keys_out, values_out = ([], [], [])
    query_blocks = query_all.reshape(block_count, block_rows, head_size)
    grad_blocks = jnp.moveaxis(grad_cols.reshape(head_size, block_count, block_rows), 1, 0)

    def visit(carried, blocks):
        keys_acc, values_acc = carried
        query_blk, grad_blk = blocks
        scores = (
            jnp.einsum("qd,kd->qk", query_blk, keys_all, preferred_element_type=jnp.float32)
            * factor
        )
        scores = scores - jnp.max(scores, axis=-1, keepdims=True)
        weights = jnp.exp(scores)
        probs = weights / jnp.sum(weights, axis=-1, keepdims=True)
        dprobs = jnp.einsum("dq,kd->qk", grad_blk, values_all, preferred_element_type=jnp.float32)
        delta = jnp.sum(probs * dprobs, axis=-1, keepdims=True)
        dscores = probs * (dprobs - delta)
        probs_low = probs.astype(jnp.bfloat16)
        dscores_low = dscores.astype(jnp.bfloat16)
        values_acc = values_acc + jnp.einsum(
            "qk,dq->kd", probs_low, grad_blk, preferred_element_type=jnp.float32
        )
        keys_acc = keys_acc + jnp.einsum(
            "qk,qd->kd", dscores_low, query_blk, preferred_element_type=jnp.float32
        )
        query_grad = (
            jnp.einsum("qk,kd->qd", dscores_low, keys_all, preferred_element_type=jnp.float32)
            * factor
        ).astype(jnp.bfloat16)
        return ((keys_acc, values_acc), query_grad)

    empty = jnp.zeros((total_rows, head_size), jnp.float32)
    (keys_acc, values_acc), query_grads = lax.scan(
        visit, (empty, empty), (query_blocks, grad_blocks)
    )
    query_out.append(query_grads.reshape(total_rows, head_size))
    keys_out.append((keys_acc * factor).astype(jnp.bfloat16))
    values_out.append(values_acc.astype(jnp.bfloat16))
    return (query_out[0], keys_out[0], values_out[0])


def on_device(
    grad_out,
    block_input,
    skip_saved,
    saved_qkv,
    out_weight,
    qkv_weight,
    gate,
    norm_scale,
    skip_gain,
):
    seq_count = lax.axis_size(SEQ)
    incoming_gradient = grad_out[0]
    tok_rows, features = incoming_gradient.shape
    local_width = out_weight.shape[1]
    head_size = HEAD_DIM
    feat_group = features // seq_count
    gated = (incoming_gradient.astype(jnp.float32) * gate[0]).astype(jnp.bfloat16)
    weight_out = out_weight[0]
    rows_in = lax.all_gather(gated, SEQ, axis=0, tiled=True)
    row_count = rows_in.shape[0]
    terms = jnp.einsum(
        "rgs,hgs->ghr",
        rows_in.reshape(row_count, seq_count, feat_group),
        weight_out.reshape(local_width, seq_count, feat_group),
        preferred_element_type=jnp.float32,
    )
    rounded = lax.optimization_barrier(terms.astype(jnp.bfloat16))
    grad_cols = jnp.sum(rounded.astype(jnp.float32), axis=0).astype(jnp.bfloat16)
    query_grad, keys_grad, values_grad = local_attention(
        saved_qkv[0, 0], saved_qkv[0, 1], saved_qkv[0, 2], grad_cols, head_size
    )
    weight_qkv = qkv_weight[0]
    total = jnp.dot(query_grad, weight_qkv[0], preferred_element_type=jnp.float32)
    total = total + jnp.dot(keys_grad, weight_qkv[1], preferred_element_type=jnp.float32)
    total = total + jnp.dot(values_grad, weight_qkv[2], preferred_element_type=jnp.float32)
    normed_grad = sum_by_axis(total, SEQ)
    xvalue = block_input[0].astype(jnp.float32)
    mean_x = jnp.mean(xvalue, axis=-1, keepdims=True)
    centered_input = xvalue - mean_x
    var_x = jnp.mean(centered_input * centered_input, axis=-1, keepdims=True)
    inverse_deviation = 1.0 / jnp.sqrt(var_x + norm_eps)
    normalized_input = centered_input * inverse_deviation
    scaled_gradient = normed_grad * (1.0 + norm_scale[0])
    input_gradient = incoming_gradient.astype(jnp.float32) + inverse_deviation * (
        scaled_gradient
        - jnp.mean(scaled_gradient, axis=-1, keepdims=True)
        - normalized_input * jnp.mean(scaled_gradient * normalized_input, axis=-1, keepdims=True)
    )
    hand_grad = input_gradient.astype(jnp.bfloat16)
    next_grad = passed_along(hand_grad, "section", 1)
    last_flag = jnp.where(
        lax.axis_index("section") == lax.axis_size("section") - 1, 1.0, 0.0
    ).astype(jnp.float32)
    down_grad = ((skip_gain[0] + last_flag) * input_gradient).astype(jnp.bfloat16)
    gain_local = jnp.sum(input_gradient * skip_saved[0].astype(jnp.float32), axis=0)
    gain_grad = taken_together(gain_local, SEQ)
    return (next_grad[None], down_grad[None], gain_grad[None])


def solution(mesh):
    torus = Mesh(mesh.devices.reshape(mesh.shape["section"], 8, 2), ("section", "seq_0", "seq_1"))
    in_specs = (
        P("section", SEQ, None),
        P("section", SEQ, None),
        P("section", SEQ, None),
        P("section", None, None, SEQ),
        P("section", SEQ, None),
        P("section", None, SEQ, None),
        P("section", None),
        P("section", None),
        P("section", None),
    )
    out_specs = (P("section", SEQ, None), P("section", SEQ, None), P("section", None))
    return jax.shard_map(
        on_device, mesh=torus, in_specs=in_specs, out_specs=out_specs, check_vma=False
    )
```

profile of v0, /device:TPU:2, one launch (start us, length us, event | category | flops | bytes accessed | tf_op | source)
XLA Modules:
  0.0 464.8 jit_solution(5071917297979454909)
XLA Ops:
  7.2 0.0 all-gather.2.cloned.1.call-start
  7.2 2.0 fusion.30
  9.2 0.0 all-gather.2.cloned.1.call-update
  9.2 0.0 reduce-scatter.3.cloned.1.call-start
  9.3 1.1 copy.29
  10.5 2.3 slice_bitcast_fusion
  12.7 182.6 %all-gather.2.cloned.1.call-done = bf16[2048,2048]{1,0:T(8,128)(2,1)} async-done(((bf16[128,2048]{1,0:T(8,128)(2,1)}), bf16[2048,2048]{1,0:T(8,128)(2,1)}) %all-gather.2.cloned.1.call-update) | async-done | bytes 8388624 | tf_op jit(solution)/shard_map/all_gather | solution.py:101
  195.3 12.3 %copy.21 = bf16[2048,2048]{0,1:T(8,128)(2,1)} copy(bf16[2048,2048]{1,0:T(8,128)(2,1)} %all-gather.2.cloned.1.call-done) | data formatting | bytes 16777216 | tf_op jit(solution)/shard_map/all_gather | solution.py:101
  207.6 9.1 %convert_bitcast_fusion = bf16[16,128,2048]{1,2,0:T(8,128)(2,1)} fusion(bf16[2048,16,128]{0,2,1:T(8,128)(2,1)} %bitcast.109, bf16[128,16,128]{2,1,0:T(8,128)(2,1)S(1)} %bitcast.111), kind=kOutput, calls=%fused_computation.28 | convolution fusion | flops 1077936128 | bytes 17301504 | tf_op jit(solution)/shard_map/rgs,hgs->ghr/dot_general | solution.py:103
  216.8 5.6 %reduce_sum.86 = bf16[128,2048]{0,1:T(8,128)(2,1)} reduce(bf16[16,128,2048]{1,2,0:T(8,128)(2,1)} %convert_bitcast_fusion, bf16[]{:T(256)} %constant.28.clone.1), dimensions={0}, to_apply=%region_2.3 | reduce | flops 3932160 | bytes 8912898 | tf_op jit(solution)/shard_map/reduce_sum | solution.py:110
  222.4 54.4 %while.15 = (s32[]{:T(128)}, f32[2048,128]{1,0:T(8,128)S(1)}, f32[2048,128]{1,0:T(8,128)S(1)}, bf16[4,512,128]{2,1,0:T(8,128)(2,1)}, bf16[4,512,128]{2,1,0:T(8,1...) while((s32[]{:T(128)}, f32[2048,128]{1,0:T(8,128)S(1)}, ...), condition=%wide.region_7.8_spmd.clone, body=%wide.region_3.7_spmd.clone.sunk | while | flops 1364326912 | bytes 77749960 | solution.py:73
  222.4 0.8 multiply_reduce_fusion.4
  223.2 1.9 copy-done
  225.1 0.8 fusion.71
  225.9 0.0 copy-start.9
  225.9 3.8 convolution_add_fusion.5
  229.8 2.2 multiply_reduce_fusion.5
  232.0 1.4 multiply_convert_fusion.5
  233.4 1.2 convolution_add_fusion.4
  234.6 1.4 fusion.72
  236.0 0.8 multiply_reduce_fusion.4
  236.8 1.9 copy-done
  238.7 0.8 fusion.71
  239.5 3.8 convolution_add_fusion.5
  243.4 2.2 multiply_reduce_fusion.5
  245.6 1.4 multiply_convert_fusion.5
  247.0 1.2 convolution_add_fusion.4
  248.2 1.4 fusion.72
  249.6 0.8 multiply_reduce_fusion.4
  250.4 1.9 copy-done
  252.3 0.8 fusion.71
  253.1 3.8 convolution_add_fusion.5
  257.0 2.2 multiply_reduce_fusion.5
  259.2 1.4 multiply_convert_fusion.5
  260.6 1.2 convolution_add_fusion.4
  261.8 1.4 fusion.72
  263.2 0.8 multiply_reduce_fusion.4
  263.9 1.9 copy-done
  265.9 0.8 fusion.71
  266.7 3.8 convolution_add_fusion.5
  270.6 2.2 multiply_reduce_fusion.5
  272.8 1.4 multiply_convert_fusion.5
  274.2 1.2 convolution_add_fusion.4
  275.4 1.4 fusion.72
  276.7 1.0 copy-done.6
  277.7 9.2 %fusion.33 = f32[2048,2048]{1,0:T(8,128)} fusion(f32[2048,128]{1,0:T(8,128)S(1)} %get-tuple-element.48, bf16[1,3,128,2048]{3,2,1,0:T(8,128)(2,1)} %param.16), kind=kOutput, calls=%fused_computation.49 | convolution fusion | flops 1074266112 | bytes 18350080 | tf_op jit(solution)/shard_map/dot_general | solution.py:116
  286.9 9.2 %fusion.37 = f32[2048,2048]{1,0:T(8,128)} fusion(bf16[2048,128]{1,0:T(8,128)(2,1)} %bitcast.11, bf16[1,3,128,2048]{3,2,1,0:T(8,128)(2,1)S(1)} %copy-done.4), kind=kOutput, calls=%fused_computation.53 | convolution fusion | flops 1073741824 | bytes 17825792 | tf_op jit(solution)/shard_map/dot_general | solution.py:115
  296.1 15.4 %add_convert_fusion = bf16[2048,2048]{1,0:T(8,128)(2,1)} fusion(f32[2048,2048]{1,0:T(8,128)} %fusion.37, f32[2048,2048]{1,0:T(8,128)} %fusion.33, bf16[1,3,128,2048]{3,2,1,0:T(8,128)(2,1)S(1)} %copy-done.4, f32[2048,128]{1,0:T(8,128)S(1)} %copy-done.7), kind=kOutput, calls=%fused_computation.27 | convolution fusion | flops 1086586880 | bytes 43515904 | tf_op jit(solution)/shard_map/dot_general | solution.py:117
  311.5 0.0 copy-start.3
  311.5 0.0 reduce-scatter.3.cloned.1.call-update
  311.5 0.0 reduce-scatter.5.cloned.1.call-start
  311.6 95.9 %reduce-scatter.3.cloned.1.call-done = bf16[256,2048]{1,0:T(8,128)(2,1)} async-done(((bf16[2048,2048]{1,0:T(8,128)(2,1)}), bf16[256,2048]{1,0:T(8,128)(2,1)}) %reduce-scatter.3.cloned.1.call-update) | async-done | bytes 1048592 | tf_op jit(solution)/shard_map/reduce_scatter | solution.py:17
  407.5 0.0 reduce-scatter.5.cloned.1.call-update
  407.5 0.2 convert_reduce_fusion
  407.7 0.3 fusion.29
  408.0 26.1 %reduce-scatter.5.cloned.1.call-done = bf16[128,2048]{1,0:T(8,128)(2,1)} async-done(((bf16[256,2048]{1,0:T(8,128)(2,1)}), bf16[128,2048]{1,0:T(8,128)(2,1)}) %reduce-scatter.5.cloned.1.call-update) | async-done | bytes 524304 | tf_op jit(solution)/shard_map/reduce_scatter | solution.py:17
  434.1 1.4 fusion.32
  435.5 1.8 fusion.31
  437.4 0.9 fusion.34
  438.3 1.9 collective-permute-start
  440.2 0.1 broadcast_in_dim.35
  440.3 16.5 %all_to_all.6 = f32[16,1,2048]{2,1,0:T(1,128)S(1)} all-to-all(f32[16,1,2048]{2,1,0:T(1,128)S(1)} %broadcast_in_dim.35), channel_id=1, replica_groups=mesh['section'=16,'seq_0'=8,'seq_1'=2] {'seq_0','seq_1'}, dimensions={0} | all-to-all | bytes 262144 | tf_op jit(solution)/shard_map/all_to_all | solution.py:29
  456.8 0.7 reduce_sum.90
  457.5 0.8 copy.46
  (44 shorter events, 0.1 us)
Async XLA Ops:
  7.2 188.1 %all-gather.2.cloned.1.call-start = ((), (), s32[]{:S(2)}) async-start(), calls=%async_computation.3 | async-start | bytes 8912896 | tf_op jit(solution)/shard_map/all_gather | solution.py:101
  9.2 398.3 %reduce-scatter.3.cloned.1.call-start = ((), (), s32[]{:S(2)}) async-start(), calls=%async_computation.4 | async-start | bytes 9437184 | tf_op jit(solution)/shard_map/reduce_scatter | solution.py:17
  216.8 5.6 %copy-start.5 = (f32[2048,128]{1,0:T(8,128)S(1)}, f32[2048,128]{1,0:T(8,128)}, u32[]{:S(2)}) copy-start(f32[2048,128]{1,0:T(8,128)} %custom-call.1) | copy-start | bytes 3145732
  223.2 1.9 copy-start
  225.9 3.9 copy-start.1
  225.9 3.9 copy-start.9
  236.8 1.9 copy-start
  239.5 3.9 copy-start.1
  239.5 3.9 copy-start.9
  250.3 1.9 copy-start
  253.1 3.9 copy-start.1
  253.1 3.9 copy-start.9
  263.9 1.9 copy-start
  266.7 3.9 copy-start.1
  266.7 3.9 copy-start.9
  276.7 1.0 copy-start.6
  277.7 9.2 %copy-start.4 = (bf16[1,3,128,2048]{3,2,1,0:T(8,128)(2,1)S(1)}, bf16[1,3,128,2048]{3,2,1,0:T(8,128)(2,1)}, u32[]{:S(2)}) copy-start(bf16[1,3,128,2048]{3,2,1,0:T(8,128)(2,1)} %param.16) | copy-start | bytes 4718596
  286.9 9.2 %copy-start.7 = (f32[2048,128]{1,0:T(8,128)S(1)}, f32[2048,128]{1,0:T(8,128)}, u32[]{:S(2)}) copy-start(f32[2048,128]{1,0:T(8,128)} %copy-done.6) | copy-start | bytes 3145732
  311.5 96.0 %copy-start.2 = (bf16[1,128,2048]{2,1,0:T(8,128)(2,1)S(1)}, bf16[1,128,2048]{2,1,0:T(8,128)(2,1)}, u32[]{:S(2)}) copy-start(bf16[1,128,2048]{2,1,0:T(8,128)(2,1)} %param.12) | copy-start | bytes 1572868
  311.5 96.5 %copy-start.10 = (f32[1,2048]{1,0:T(1,128)S(1)}, f32[1,2048]{1,0:T(1,128)}, u32[]{:S(2)}) copy-start(f32[1,2048]{1,0:T(1,128)} %param.18) | copy-start | bytes 24580
  311.5 96.5 %copy-start.11 = (f32[1,2048]{1,0:T(1,128)S(1)}, f32[1,2048]{1,0:T(1,128)}, u32[]{:S(2)}) copy-start(f32[1,2048]{1,0:T(1,128)} %param.19) | copy-start | bytes 24580
  311.5 124.0 %copy-start.3 = (bf16[1,128,2048]{2,1,0:T(8,128)(2,1)S(1)}, bf16[1,128,2048]{2,1,0:T(8,128)(2,1)}, u32[]{:S(2)}) copy-start(bf16[1,128,2048]{2,1,0:T(8,128)(2,1)} %param.11) | copy-start | bytes 1572868
  311.5 124.0 %copy-start.8 = (bf16[1,128,2048]{2,1,0:T(8,128)(2,1)S(1)}, bf16[1,128,2048]{2,1,0:T(8,128)(2,1)}, u32[]{:S(2)}) copy-start(bf16[1,128,2048]{2,1,0:T(8,128)(2,1)} %param.13) | copy-start | bytes 1572868
  311.5 122.6 %reduce-scatter.5.cloned.1.call-start = ((), (), s32[]{:S(2)}) async-start(), calls=%async_computation.5 | async-start | bytes 1572864 | tf_op jit(solution)/shard_map/reduce_scatter | solution.py:17
  438.3 19.2 %collective-permute-start = (bf16[128,2048]{1,0:T(8,128)(2,1)S(1)}, bf16[128,2048]{1,0:T(8,128)(2,1)S(1)}, u32[]{:S(2)}, u32[]{:S(2)}) collective-permute-start(bf16[128,2048]{1,0:T(8,128)(2,1)S(1)} %get-tuple-element.129), channel_id=1, source_target_pairs={{0,16},{16,32},{32,48},{48,64},{64,80},{80,96},{96,112},{112,128},... | collective-permute-start | bytes 1572872 | tf_op jit(solution)/shard_map/ppermute | solution.py:24
Sparse Core Ops, SparseCore 0:
  9.8 185.4 all-gather.1
  311.7 95.7 reduce-scatter.2
  410.0 24.0 reduce-scatter.4
where the time goes:
time: 468 us; the launch traced here: 465 us
  waiting for transfers between devices  305 us (65%)
  matrix products  80.4 us (17%)
  local copies, waits for them, and re-layouts  25.4 us (5%)
  other arithmetic  21.8 us (5%)
  blocking collectives  16.5 us (4%)
  between operations  13.9 us (3%)
    all_gather x1, waiting for transfers between devices, on_device(): rows_in = lax.all_gather(gated, SEQ, axis=0, tiled=True)  183 us
    reduce_scatter x2, waiting for transfers between devices, sum_by_axis(): running = lax.psum_scatter(running, axis, scatter_dimension=0, tiled=True)  122 us
    all_to_all x1, blocking collectives, copy_for_each(): return lax.all_to_all(copies, axis, split_axis=0, concat_axis=0, tiled=True)  16.5 us
    dot_general x1, matrix products, on_device(): jnp.dot(values_grad, weight_qkv[2], preferred_element_type=jnp.float32)  15.4 us
    dot_general x4, matrix products, visit(): jnp.einsum('qk,dq->kd', probs_low, grad_blk, preferred_element_type=jnp.f...  15.3 us
    all_gather x1, local copies, waits for them, and re-layouts, on_device(): rows_in = lax.all_gather(gated, SEQ, axis=0, tiled=True)  12.3 us
  transfers between devices with their start and end apart: 4, of which 3 were waited for; matrix products, arithmetic and copies ran while one was open for 1% of the time, Pallas kernels for 0%

commit v1 on v0

v1 whole, which is shorter than its diff:
```python
import functools

import jax
import jax.numpy as jnp
from jax import lax
from jax.experimental import pallas as pl
from jax.experimental.pallas import tpu as pltpu
from jax.sharding import PartitionSpec as P

F32 = jnp.float32
BF16 = jnp.bfloat16
MESH = pl.DeviceIdType.MESH

HD = 128
NZ = 8
SH = 128
D = 2048
T = 2048
KC = 256
NKC = T // KC
QR = 32
EPS = 1e-6
FACTOR = HD**-0.5


def mul_t(a, b):
    return lax.dot_general(a, b, (((1,), (1,)), ((), ())), preferred_element_type=F32)


def mul(a, b):
    return jnp.dot(a, b, preferred_element_type=F32)


def kernel(
    nsec,
    go_ref,
    bi_ref,
    sk_ref,
    qkv_ref,
    wo_ref,
    wq_ref,
    gate_ref,
    scale_ref,
    gain_ref,
    next_ref,
    down_ref,
    gg_ref,
    go_v,
    bi_v,
    sk_v,
    qkv_v,
    w2,
    wcat,
    gath,
    sbuf,
    pbuf,
    obuf,
    kt,
    vt,
    vaug,
    gblk,
    gsend,
    dk_acc,
    dv_acc,
    xx,
    xpar,
    ybuf,
    rsend,
    rrecv,
    xhat,
    rstd_v,
    hand,
    down_v,
    gslots,
    ld_sem,
    ag_s,
    ag_r,
    wo_s,
    wo_r,
    wq_s,
    wq_r,
    g_s,
    g_r,
    x_s,
    x_r,
    rs_s,
    rs_r,
    nx_s,
    nx_r,
    dn_sem,
    gg_s,
    gg_r,
):
    sec = lax.axis_index("section")
    me = lax.axis_index("seq")
    z = lax.div(me, 2)
    y = lax.rem(me, 2)

    def zmod(v):
        return lax.rem(v + 2 * NZ, NZ)

    def dev(zz, yy):
        return (sec, zz * 2 + yy)

    z_to = (dev(zmod(z + 1), y), dev(zmod(z - 1), y))
    partner = dev(z, 1 - y)

    loads = [
        pltpu.make_async_copy(src, dst, ld_sem.at[i])
        for i, (src, dst) in enumerate(
            [
                (go_ref, go_v),
                (qkv_ref, qkv_v),
                (wo_ref, w2.at[pl.ds(0, SH)]),
                (wq_ref, wcat.at[pl.ds(0, 3)]),
                (bi_ref, bi_v),
                (sk_ref, sk_v),
            ]
        )
    ]
    for copy in loads:
        copy.start()

    barrier = pltpu.get_barrier_semaphore()

    @pl.loop(1, 2 * NZ)
    def _(off):
        pl.semaphore_signal(
            barrier, inc=1, device_id=(sec, lax.rem(me + off, 2 * NZ)), device_id_type=MESH
        )

    greeted = 2 * NZ - 1
    if nsec > 1:
        for step in (1, nsec - 1):
            pl.semaphore_signal(
                barrier, inc=1, device_id=(lax.rem(sec + step, nsec), me), device_id_type=MESH
            )
        greeted += 2

    loads[0].wait()
    gath[z] = (go_v[...].astype(F32) * gate_ref[...]).astype(BF16)
    pl.semaphore_wait(barrier, greeted)

    def ag_copy(way, pos, shard):
        half = lax.rem(pos, 2) if way == 0 else 1 - lax.rem(pos, 2)
        part = gath.at[shard, pl.ds(pl.multiple_of(half * (SH // 2), SH // 2), SH // 2)]
        return pltpu.make_async_remote_copy(
            src_ref=part,
            dst_ref=part,
            send_sem=ag_s.at[way, pos],
            recv_sem=ag_r.at[way, pos],
            device_id=z_to[way],
            device_id_type=MESH,
        )

    def ag_out(way, pos):
        back = lax.div(pos, 2)
        return ag_copy(way, pos, zmod(z - back) if way == 0 else zmod(z + back))

    def ag_in(way, pos):
        back = lax.div(pos, 2) + 1
        return ag_copy(way, pos, zmod(z - back) if way == 0 else zmod(z + back))

    for pos in (0, 1):
        for way in (0, 1):
            ag_out(way, jnp.int32(pos)).start()

    def forward(pos):
        for way in (0, 1):
            ag_in(way, pos).wait_recv()
            ag_out(way, pos + 2).start()

    wo_copy = pltpu.make_async_remote_copy(
        src_ref=wo_ref,
        dst_ref=w2.at[pl.ds(SH, SH)],
        send_sem=wo_s,
        recv_sem=wo_r,
        device_id=partner,
        device_id_type=MESH,
    )
    wo_copy.start()

    def wq_copy(i):
        which = lax.div(i, 2)
        rows = pl.ds(pl.multiple_of(lax.rem(i, 2) * 64, 64), 64)
        return pltpu.make_async_remote_copy(
            src_ref=wq_ref.at[which, rows],
            dst_ref=wcat.at[3 + which, rows],
            send_sem=wq_s.at[i],
            recv_sem=wq_r.at[i],
            device_id=partner,
            device_id_type=MESH,
        )

    loads[1].wait()
    lanes = lax.broadcasted_iota(jnp.int32, (KC, HD), 1)
    eye = (
        lax.broadcasted_iota(jnp.int32, (HD, HD), 0)
        == lax.broadcasted_iota(jnp.int32, (HD, HD), 1)
    ).astype(F32).astype(BF16)
    ones2 = (lanes < 2).astype(F32).astype(BF16)

    @pl.loop(0, NKC)
    def _(c):
        rows = pl.ds(pl.multiple_of(c * KC, KC), KC)
        kk = qkv_v[1, rows]
        vv = qkv_v[2, rows]
        kt[c] = mul_t(eye, kk).astype(BF16)
        vt[c] = mul_t(eye, vv).astype(BF16)
        vaug[rows, pl.ds(0, HD)] = vv
        vaug[rows, pl.ds(HD, HD)] = ones2

    def block_of(b):
        d = lax.div(b + 1, 2)
        odd = lax.rem(b, 2)
        far1 = (1 - odd) * lax.div(b + 6, 7)
        far2 = 1 - odd * (1 - lax.div(b, 7))
        return (zmod(z + d), far1), (zmod(z - d), far2)

    def token_rows(zz, far):
        shard = zz * 2 + lax.rem(y + far, 2)
        return pl.ds(pl.multiple_of(shard * SH, SH), SH)

    def queries(b):
        one, two = block_of(b)
        return jnp.concatenate([qkv_v[0, token_rows(*one)], qkv_v[0, token_rows(*two)]], axis=0)

    def softmax_block(b):
        qb = queries(b)

        def scores(c, top):
            rows = pl.ds(pl.multiple_of(c * KC, KC), KC)
            s = mul_t(qkv_v[1, rows], qb)
            sbuf[rows, :] = s
            return jnp.maximum(top, s.reshape(KC // 8, 8, 256).max(axis=0))

        top = lax.fori_loop(0, NKC, scores, jnp.full((8, 256), -jnp.inf, F32))
        top = jnp.max(top, axis=0, keepdims=True)

        def weights(c, total):
            rows = pl.ds(pl.multiple_of(c * KC, KC), KC)
            e = jnp.exp((sbuf[rows, :] - top) * FACTOR)
            sbuf[rows, :] = e
            return total + e.reshape(KC // 8, 8, 256).sum(axis=0)

        total = lax.fori_loop(0, NKC, weights, jnp.zeros((8, 256), F32))
        inverse = 1.0 / jnp.sum(total, axis=0, keepdims=True)

        def output(c, acc):
            rows = pl.ds(pl.multiple_of(c * KC, KC), KC)
            p = (sbuf[rows, :] * inverse).astype(BF16)
            pbuf[b, rows, :] = p
            return acc + mul(vt[c], p)

        out_t = lax.fori_loop(0, NKC, output, jnp.zeros((HD, 256), F32))
        obuf[b] = out_t.T

    dk_acc[...] = jnp.zeros_like(dk_acc)
    dv_acc[...] = jnp.zeros_like(dv_acc)

    def start_wq(i):
        wq_copy(jnp.int32(i)).start()

    @pl.loop(0, 3)
    def _(b):
        softmax_block(b)

    forward(jnp.int32(0))
    start_wq(0)

    @pl.loop(3, 8)
    def _(b):
        softmax_block(b)

    forward(jnp.int32(1))
    start_wq(1)

    def g_copy(d, two):
        if two:
            src, dst = gsend.at[d], gblk.at[2 * d]
        else:
            blk = 0 if d == 0 else 7
            src, dst = gsend.at[d, pl.ds(0, SH)], gblk.at[blk, pl.ds(SH, SH)]
        return pltpu.make_async_remote_copy(
            src_ref=src,
            dst_ref=dst,
            send_sem=g_s.at[d],
            recv_sem=g_r.at[d],
            device_id=partner,
            device_id_type=MESH,
        )

    def backward_block(b):
        qb = queries(b)
        g = gblk[b]
        delta = jnp.sum(g.astype(F32) * obuf[b], axis=1, keepdims=True)
        high = delta.astype(BF16).astype(F32)
        low = delta - high
        extra = jnp.where(lanes == 0, -high, jnp.where(lanes == 1, -low, 0.0)).astype(BF16)
        gaug = jnp.concatenate([g, extra], axis=1)

        def step(c, dq_t):
            rows = pl.ds(pl.multiple_of(c * KC, KC), KC)
            p = pbuf[b, rows, :]
            ds = (p.astype(F32) * mul_t(vaug[rows, :], gaug)).astype(BF16)
            dk_acc[rows, :] += mul(ds, qb)
            dv_acc[rows, :] += mul(p, g)
            return dq_t + mul(kt[c], ds)

        dq_t = lax.fori_loop(0, NKC, step, jnp.zeros((HD, 256), F32))
        dq = (dq_t.T * FACTOR).astype(BF16)
        one, two = block_of(b)
        xx[one[1], one[0], :, pl.ds(0, HD)] = dq[:SH]
        xx[two[1], two[0], :, pl.ds(0, HD)] = dq[SH:]

    loads[2].wait()
    wo_copy.wait_recv()

    def single(d):
        res = mul_t(gath[zmod(z + d)], w2[...]).astype(BF16)
        blk = 0 if d == 0 else 7
        gsend[d, pl.ds(0, SH)] = res[:, HD:]
        g_copy(d, False).start()
        gblk[blk, pl.ds(0, SH)] = res[:, :HD]
        g_copy(d, False).wait_recv()
        backward_block(jnp.int32(blk))

    single(0)

    def pair(d):
        both = jnp.concatenate([gath[zmod(z + d)], gath[zmod(z - d)]], axis=0)
        res = mul_t(both, w2[...]).astype(BF16)
        gsend[d] = res[:, HD:]
        g_copy(d, True).start()
        gblk[2 * d - 1] = res[:, :HD]
        backward_block(2 * d - 1)
        g_copy(d, True).wait_recv()
        backward_block(2 * d)

    @pl.loop(1, 4)
    def _(d):
        pair(d)
        wq_copy(d + 1).start()

        @pl.when(d == 1)
        def _():
            wq_copy(jnp.int32(5)).start()

        @pl.when(d < 3)
        def _():
            forward(2 * d)

        @pl.when(d == 1)
        def _():
            forward(jnp.int32(3))

        @pl.when(d == 2)
        def _():
            for way in (0, 1):
                ag_in(way, jnp.int32(5)).wait_recv()

        @pl.when(d == 3)
        def _():
            for way in (0, 1):
                ag_in(way, jnp.int32(6)).wait_recv()

    single(4)

    def x_copy(zz):
        return pltpu.make_async_remote_copy(
            src_ref=xx.at[1, zz],
            dst_ref=xpar.at[zz],
            send_sem=x_s.at[zz],
            recv_sem=x_r.at[zz],
            device_id=partner,
            device_id_type=MESH,
        )

    def place(zz, far):
        rows = token_rows(zz, far)
        xx[far, zz, :, pl.ds(HD, HD)] = (dk_acc[rows, :] * FACTOR).astype(BF16)
        xx[far, zz, :, pl.ds(2 * HD, HD)] = dv_acc[rows, :].astype(BF16)

    def in_order(i):
        away = 4 - lax.div(i + 1, 2)
        return zmod(z + away * (2 * lax.rem(i, 2) - 1))

    @pl.loop(0, NZ)
    def _(i):
        zz = in_order(i)
        place(zz, 1)
        x_copy(zz).start()

    @pl.loop(0, NZ)
    def _(i):
        place(in_order(i), 0)

    loads[3].wait()

    @pl.loop(0, 6)
    def _(i):
        wq_copy(i).wait_recv()

    def shard_x(zz):
        return jnp.concatenate([xx[0, zz], xpar[zz]], axis=1)

    def product(x, rows):
        @pl.loop(0, D // 512)
        def _(n):
            cols = pl.ds(pl.multiple_of(n * 512, 512), 512)
            w = wcat[:, :, cols].reshape(6 * HD, 512)
            ybuf[pl.ds(0, rows), cols] = mul(x, w)

    def rs_copy(way, pos):
        return pltpu.make_async_remote_copy(
            src_ref=rsend.at[way, pos],
            dst_ref=rrecv.at[way, pos],
            send_sem=rs_s.at[way, pos],
            recv_sem=rs_r.at[way, pos],
            device_id=z_to[way],
            device_id_type=MESH,
        )

    def piece(way, k):
        q = lax.rem(k, 2) if way else 1 - lax.rem(k, 2)
        return 2 * q + lax.div(k, 2)

    far4 = zmod(z + 4)
    x_copy(far4).wait_recv()
    product(shard_x(far4), SH)
    for k in (0, 1):
        for way in (0, 1):
            rsend[way, k] = ybuf[pl.ds((2 * way + k) * QR, QR), :].astype(BF16)
            rs_copy(way, k).start()

    loads[4].wait()
    loads[5].wait()

    @pl.loop(0, SH // QR)
    def _(i):
        rows = pl.ds(pl.multiple_of(i * QR, QR), QR)
        xv = bi_v[rows, :].astype(F32)
        centered = xv - jnp.mean(xv, axis=-1, keepdims=True)
        var = jnp.mean(centered * centered, axis=-1, keepdims=True)
        rstd = 1.0 / jnp.sqrt(var + EPS)
        xhat[rows, :] = centered * rstd
        rstd_v[rows, :] = jnp.broadcast_to(rstd, (QR, HD))

    def pair_product(d):
        plus, minus = zmod(z + d), zmod(z - d)
        x_copy(plus).wait_recv()
        x_copy(minus).wait_recv()
        product(jnp.concatenate([shard_x(plus), shard_x(minus)], axis=0), 2 * SH)

    def rows_of(way, k):
        return pl.ds(pl.multiple_of(way * SH + piece(way, k) * QR, QR), QR)

    def send_fresh(k):
        for way in (0, 1):
            rsend[way, 2 + k] = ybuf[rows_of(way, k), :].astype(BF16)
            rs_copy(way, 2 + k).start()

    def send_added(pos, k, came):
        for way in (0, 1):
            rs_copy(way, came).wait_recv()
            rsend[way, pos] = (ybuf[rows_of(way, k), :] + rrecv[way, came].astype(F32)).astype(BF16)
            rs_copy(way, pos).start()

    pair_product(3)
    for k in range(4):
        if k % 2 == 0:
            send_fresh(k)
        else:
            send_added(2 + k, k, k // 2)

    @pl.loop(1, 3)
    def _(s):
        pair_product(3 - s)

        @pl.loop(0, 4)
        def _(k):
            pos = 2 + 4 * s + k
            send_added(pos, k, pos - 4)

    x_copy(z).wait_recv()
    product(shard_x(z), SH)

    last = jnp.where(sec == nsec - 1, 1.0, 0.0).astype(F32)
    one_scale = 1.0 + scale_ref[...]
    down_gain = gain_ref[...] + last

    def next_copy(q):
        rows = pl.ds(pl.multiple_of(q * QR, QR), QR)
        return pltpu.make_async_remote_copy(
            src_ref=hand.at[rows],
            dst_ref=next_ref.at[rows],
            send_sem=nx_s.at[q],
            recv_sem=nx_r.at[q],
            device_id=(lax.rem(sec + 1, nsec), me),
            device_id_type=MESH,
        )

    def down_copy(q):
        rows = pl.ds(pl.multiple_of(q * QR, QR), QR)
        return pltpu.make_async_copy(down_v.at[rows], down_ref.at[rows], dn_sem.at[q])

    def finish(q, plus_pos, minus_pos):
        rows = pl.ds(pl.multiple_of(q * QR, QR), QR)
        normed = ybuf[rows, :] + rrecv[0, plus_pos].astype(F32) + rrecv[1, minus_pos].astype(F32)
        xh = xhat[rows, :]
        scaled = normed * one_scale
        mean1 = jnp.mean(scaled, axis=-1, keepdims=True)
        mean2 = jnp.mean(scaled * xh, axis=-1, keepdims=True)
        rstd = rstd_v[rows, pl.ds(0, 1)]
        ig = go_v[rows, :].astype(F32) + rstd * (scaled - mean1 - xh * mean2)
        hand[rows, :] = ig.astype(BF16)
        if nsec > 1:

            @pl.when(sec < nsec - 1)
            def _():
                next_copy(q).start()

        down_v[rows, :] = (down_gain * ig).astype(BF16)
        down_copy(q).start()
        return jnp.sum(ig * sk_v[rows, :].astype(F32), axis=0, keepdims=True)

    gain_sum = jnp.zeros((1, D), F32)
    for j in (0, 1):
        for k in (2 * j, 2 * j + 1):
            for way in (0, 1):
                rs_copy(way, jnp.int32(10 + k)).wait_recv()
        gain_sum += finish(jnp.int32(j), 10 + 2 * j + 1, 10 + 2 * j)
        gain_sum += finish(jnp.int32(2 + j), 10 + 2 * j, 10 + 2 * j + 1)

    gslots[me] = gain_sum

    def gain_copy(off):
        return pltpu.make_async_remote_copy(
            src_ref=gslots.at[me],
            dst_ref=gslots.at[me],
            send_sem=gg_s.at[off],
            recv_sem=gg_r.at[off],
            device_id=(sec, lax.rem(me + off, 2 * NZ)),
            device_id_type=MESH,
        )

    def gain_in(off):
        came = lax.rem(me - off + 2 * NZ, 2 * NZ)
        return pltpu.make_async_remote_copy(
            src_ref=gslots.at[came],
            dst_ref=gslots.at[came],
            send_sem=gg_s.at[off],
            recv_sem=gg_r.at[off],
            device_id=(sec, lax.rem(me + off, 2 * NZ)),
            device_id_type=MESH,
        )

    @pl.loop(1, 2 * NZ)
    def _(off):
        gain_copy(off).start()

    @pl.loop(0, 7)
    def _(pos):
        for way in (0, 1):
            ag_out(way, pos).wait_send()

    if nsec > 1:

        @pl.when(sec == 0)
        def _():
            gath[0] = jnp.zeros((SH, D), BF16)
            zero = pltpu.make_async_copy(gath.at[0], next_ref, nx_r.at[0])
            zero.start()
            zero.wait()

    @pl.loop(1, 2 * NZ)
    def _(off):
        gain_in(off).wait_recv()

    gg_ref[...] = jnp.sum(gslots[...], axis=0)

    wo_copy.wait_send()

    @pl.loop(0, 6)
    def _(i):
        wq_copy(i).wait_send()

    for d in range(5):
        g_copy(d, 0 < d < 4).wait_send()

    @pl.loop(0, NZ)
    def _(i):
        x_copy(i).wait_send()

    @pl.loop(0, 14)
    def _(pos):
        for way in (0, 1):
            rs_copy(way, pos).wait_send()

    @pl.loop(0, 4)
    def _(q):
        down_copy(q).wait()

    @pl.loop(1, 2 * NZ)
    def _(off):
        gain_copy(off).wait_send()

    if nsec > 1:

        @pl.when(sec < nsec - 1)
        def _():
            @pl.loop(0, 4)
            def _(q):
                next_copy(q).wait_send()

        @pl.when(sec > 0)
        def _():
            @pl.loop(0, 4)
            def _(q):
                next_copy(q).wait_recv()


def on_device(nsec, go, bi, sk, qkv, wo, wq, gate, scale, gain):
    any_spec = pl.BlockSpec(memory_space=pl.ANY)
    vmem_spec = pl.BlockSpec(memory_space=pltpu.VMEM)
    dma = pltpu.SemaphoreType.DMA
    nxt, down, gg = pl.pallas_call(
        functools.partial(kernel, nsec),
        out_shape=(
            jax.ShapeDtypeStruct((SH, D), BF16),
            jax.ShapeDtypeStruct((SH, D), BF16),
            jax.ShapeDtypeStruct((1, D), F32),
        ),
        in_specs=[any_spec] * 6 + [vmem_spec] * 3,
        out_specs=(any_spec, any_spec, vmem_spec),
        scratch_shapes=[
            pltpu.VMEM((SH, D), BF16),
            pltpu.VMEM((SH, D), BF16),
            pltpu.VMEM((SH, D), BF16),
            pltpu.VMEM((3, T, HD), BF16),
            pltpu.VMEM((2 * SH, D), BF16),
            pltpu.VMEM((6, HD, D), BF16),
            pltpu.VMEM((NZ, SH, D), BF16),
            pltpu.VMEM((T, 256), F32),
            pltpu.VMEM((8, T, 256), BF16),
            pltpu.VMEM((8, 256, HD), F32),
            pltpu.VMEM((NKC, HD, KC), BF16),
            pltpu.VMEM((NKC, HD, KC), BF16),
            pltpu.VMEM((T, 2 * HD), BF16),
            pltpu.VMEM((8, 256, HD), BF16),
            pltpu.VMEM((5, 256, HD), BF16),
            pltpu.VMEM((T, HD), F32),
            pltpu.VMEM((T, HD), F32),
            pltpu.VMEM((2, NZ, SH, 3 * HD), BF16),
            pltpu.VMEM((NZ, SH, 3 * HD), BF16),
            pltpu.VMEM((2 * SH, D), F32),
            pltpu.VMEM((2, 14, QR, D), BF16),
            pltpu.VMEM((2, 14, QR, D), BF16),
            pltpu.VMEM((SH, D), F32),
            pltpu.VMEM((SH, HD), F32),
            pltpu.VMEM((SH, D), BF16),
            pltpu.VMEM((SH, D), BF16),
            pltpu.VMEM((2 * NZ, 1, D), F32),
            dma((6,)),
            dma((2, 7)),
            dma((2, 7)),
            dma,
            dma,
            dma((6,)),
            dma((6,)),
            dma((5,)),
            dma((5,)),
            dma((NZ,)),
            dma((NZ,)),
            dma((2, 14)),
            dma((2, 14)),
            dma((4,)),
            dma((4,)),
            dma((4,)),
            dma((2 * NZ,)),
            dma((2 * NZ,)),
        ],
        compiler_params=pltpu.CompilerParams(
            collective_id=0, has_side_effects=True, vmem_limit_bytes=56 * 2**20
        ),
    )(go[0], bi[0], sk[0], qkv[0], wo[0], wq[0], gate, scale, gain)
    return nxt[None], down[None], gg


def solution(mesh):
    in_specs = (
        P("section", "seq", None),
        P("section", "seq", None),
        P("section", "seq", None),
        P("section", None, None, "seq"),
        P("section", "seq", None),
        P("section", None, "seq", None),
        P("section", None),
        P("section", None),
        P("section", None),
    )
    out_specs = (P("section", "seq", None), P("section", "seq", None), P("section", None))
    return jax.shard_map(
        functools.partial(on_device, mesh.shape["section"]),
        mesh=mesh,
        in_specs=in_specs,
        out_specs=out_specs,
        check_vma=False,
    )
```

time: 468 us -> 161 us (0.34)
  waiting for transfers between devices: 305 us -> 0 us
  Pallas kernels: 0 us -> 155 us
  matrix products: 80.4 us -> 0 us
  other arithmetic: 21.8 us -> 0 us
  local copies, waits for them, and re-layouts: 25.4 us -> 4.37 us
  blocking collectives: 16.5 us -> 0 us
  between operations: 13.9 us -> 0.65 us
    all_gather x1 -> x0, waiting for transfers between devices: 183 us -> none  [on_device(): rows_in = lax.all_gather(gated, SEQ, axis=0, tiled=True)]
    pallas_call x0 -> x1, Pallas kernels: none -> 155 us  [on_device(): pl.pallas_call(functools.partial(kernel, nsec), out_shape=(jax.ShapeDtype...]
    reduce_scatter x2 -> x0, waiting for transfers between devices: 122 us -> none  [sum_by_axis(): running = lax.psum_scatter(running, axis, scatter_dimension=0, tiled=True)]
    dot_general x24 -> x0, matrix products: 80.4 us -> none  [the longest x1 15.4 us: on_device(): jnp.dot(values_grad, weight_qkv[2], preferred_element_type=jnp.float32)]
    all_to_all x1 -> x0, blocking collectives: 16.5 us -> none  [copy_for_each(): return lax.all_to_all(copies, axis, split_axis=0, concat_axis=0, tiled=True)]
    reduce_sum x10 -> x0, other arithmetic: 13.2 us -> none  [the longest x1 5.62 us: on_device(): jnp.sum(rounded.astype(jnp.float32), axis=0).astype(jnp.bfloat16)]
    all_gather x1 -> x0, local copies, waits for them, and re-layouts: 12.3 us -> none  [on_device(): rows_in = lax.all_gather(gated, SEQ, axis=0, tiled=True)]
    while x24 -> x0, local copies, waits for them, and re-layouts: 7.75 us -> none
  transfers between devices with their start and end apart: 4 -> 0, of which waited for: 3 -> 0; matrix products, arithmetic and copies ran while one was open for 1% -> 0% of each run, Pallas kernels for 0% -> 0%
where the time goes in v1:
time: 161 us; the launch traced here: 160 us
  Pallas kernels  155 us (96%)
  local copies, waits for them, and re-layouts  4.37 us (3%)
    pallas_call x1, Pallas kernels, on_device(): pl.pallas_call(functools.partial(kernel, nsec), out_shape=(jax.ShapeDtype...  155 us
    unnamed x5, local copies, waits for them, and re-layouts  4.37 us

profile of v1, /device:TPU:2, one launch (start us, length us, event | category | flops | bytes accessed | tf_op | source)
XLA Modules:
  0.0 160.4 jit_solution(3624575672883745379)
XLA Ops:
  0.6 155.4 %shard_map.112 = (bf16[128,2048]{1,0:T(8,128)(2,1)}, bf16[128,2048]{1,0:T(8,128)(2,1)}, f32[1,2048]{1,0:T(1,128)}) custom-call(bf16[128,2048]{1,0:T(8,128)(2,1)} %bitcast.10, bf16[128,2048]{1,0:T(8,128)(2,1)} %bitcast.11, bf16[128,2048]{1,0:T(8,128)(2,1)} %bitcast.12, bf16[3,2048,128]{2,1,0:T(8,128)(2,1)} %bitcast.8, bf16[128,2048]{1,0:T(8,128)(2,1)} %bitcast.13, ...), custom_call_target="tpu_custom_call" | custom-call | tf_op jit(solution)/shard_map/pallas_call | solution.py:627
  156.0 0.0 copy-start
  156.0 1.9 %copy.15 = bf16[1,128,2048]{2,1,0:T(8,128)(2,1)} copy(bf16[1,128,2048]{2,1,0:T(8,128)(2,1)} %bitcast.15) | data formatting | bytes 1048576
  157.9 1.9 %copy.16 = bf16[1,128,2048]{2,1,0:T(8,128)(2,1)} copy(bf16[1,128,2048]{2,1,0:T(8,128)(2,1)} %bitcast.14) | data formatting | bytes 1048576
  159.8 0.0 copy-done
  159.8 0.6 copy.17
Async XLA Ops:
  156.0 3.8 %copy-start = (f32[1,2048]{1,0:T(1,128)S(1)}, f32[1,2048]{1,0:T(1,128)}, u32[]{:S(2)}) copy-start(f32[1,2048]{1,0:T(1,128)} %get-tuple-element.14) | copy-start | bytes 24580

commit v2 on v1

--- a/solution.py
+++ b/solution.py
@@ -18,6 +18,7 @@
 T = 2048
 KC = 256
 NKC = T // KC
+UN = 8
 QR = 32
 EPS = 1e-6
 FACTOR = HD**-0.5
@@ -169,6 +170,7 @@
         for way in (0, 1):
             ag_in(way, pos).wait_recv()
             ag_out(way, pos + 2).start()
+        wq_copy(pos).start()
 
     wo_copy = pltpu.make_async_remote_copy(
         src_ref=wo_ref,
@@ -234,7 +236,7 @@
             sbuf[rows, :] = s
             return jnp.maximum(top, s.reshape(KC // 8, 8, 256).max(axis=0))
 
-        top = lax.fori_loop(0, NKC, scores, jnp.full((8, 256), -jnp.inf, F32))
+        top = lax.fori_loop(0, NKC, scores, jnp.full((8, 256), -jnp.inf, F32), unroll=UN)
         top = jnp.max(top, axis=0, keepdims=True)
 
         def weights(c, total):
@@ -243,7 +245,7 @@
             sbuf[rows, :] = e
             return total + e.reshape(KC // 8, 8, 256).sum(axis=0)
 
-        total = lax.fori_loop(0, NKC, weights, jnp.zeros((8, 256), F32))
+        total = lax.fori_loop(0, NKC, weights, jnp.zeros((8, 256), F32), unroll=UN)
         inverse = 1.0 / jnp.sum(total, axis=0, keepdims=True)
 
         def output(c, acc):
@@ -252,28 +254,19 @@
             pbuf[b, rows, :] = p
             return acc + mul(vt[c], p)
 
-        out_t = lax.fori_loop(0, NKC, output, jnp.zeros((HD, 256), F32))
+        out_t = lax.fori_loop(0, NKC, output, jnp.zeros((HD, 256), F32), unroll=UN)
         obuf[b] = out_t.T
 
     dk_acc[...] = jnp.zeros_like(dk_acc)
     dv_acc[...] = jnp.zeros_like(dv_acc)
 
-    def start_wq(i):
-        wq_copy(jnp.int32(i)).start()
-
-    @pl.loop(0, 3)
+    @pl.loop(0, 8)
     def _(b):
         softmax_block(b)
 
-    forward(jnp.int32(0))
-    start_wq(0)
-
-    @pl.loop(3, 8)
-    def _(b):
-        softmax_block(b)
-
-    forward(jnp.int32(1))
-    start_wq(1)
+        @pl.when(lax.rem(b, 3) == 2)
+        def _():
+            forward(lax.div(b, 3))
 
     def g_copy(d, two):
         if two:
@@ -307,7 +300,7 @@
             dv_acc[rows, :] += mul(p, g)
             return dq_t + mul(kt[c], ds)
 
-        dq_t = lax.fori_loop(0, NKC, step, jnp.zeros((HD, 256), F32))
+        dq_t = lax.fori_loop(0, NKC, step, jnp.zeros((HD, 256), F32), unroll=UN)
         dq = (dq_t.T * FACTOR).astype(BF16)
         one, two = block_of(b)
         xx[one[1], one[0], :, pl.ds(0, HD)] = dq[:SH]
@@ -337,32 +330,24 @@
         g_copy(d, True).wait_recv()
         backward_block(2 * d)
 
+    forward(jnp.int32(2))
+
     @pl.loop(1, 4)
     def _(d):
         pair(d)
-        wq_copy(d + 1).start()
-
-        @pl.when(d == 1)
+
+        @pl.when(d < 3)
+        def _():
+            forward(d + 2)
+
+        @pl.when(d > 1)
+        def _():
+            for way in (0, 1):
+                ag_in(way, d + 3).wait_recv()
+
+        @pl.when(d == 2)
         def _():
             wq_copy(jnp.int32(5)).start()
-
-        @pl.when(d < 3)
-        def _():
-            forward(2 * d)
-
-        @pl.when(d == 1)
-        def _():
-            forward(jnp.int32(3))
-
-        @pl.when(d == 2)
-        def _():
-            for way in (0, 1):
-                ag_in(way, jnp.int32(5)).wait_recv()
-
-        @pl.when(d == 3)
-        def _():
-            for way in (0, 1):
-                ag_in(way, jnp.int32(6)).wait_recv()
 
     single(4)
 
@@ -385,11 +370,18 @@
         away = 4 - lax.div(i + 1, 2)
         return zmod(z + away * (2 * lax.rem(i, 2) - 1))
 
-    @pl.loop(0, NZ)
+    place(in_order(jnp.int32(0)), 1)
+    x_copy(in_order(jnp.int32(0))).start()
+
+    @pl.loop(1, NZ)
     def _(i):
-        zz = in_order(i)
-        place(zz, 1)
-        x_copy(zz).start()
+        place(in_order(i), 1)
+
+    def start_x(i):
+        x_copy(in_order(jnp.int32(i))).start()
+
+    start_x(1)
+    start_x(2)
 
     @pl.loop(0, NZ)
     def _(i):
@@ -427,6 +419,8 @@
 
     far4 = zmod(z + 4)
     x_copy(far4).wait_recv()
+    start_x(3)
+    start_x(4)
     product(shard_x(far4), SH)
     for k in (0, 1):
         for way in (0, 1):
@@ -450,6 +444,16 @@
         plus, minus = zmod(z + d), zmod(z - d)
         x_copy(plus).wait_recv()
         x_copy(minus).wait_recv()
+
+        @pl.when(d == 3)
+        def _():
+            start_x(5)
+            start_x(6)
+
+        @pl.when(d == 2)
+        def _():
+            start_x(7)
+
         product(jnp.concatenate([shard_x(plus), shard_x(minus)], axis=0), 2 * SH)
 
     def rows_of(way, k):
@@ -466,7 +470,7 @@
             rsend[way, pos] = (ybuf[rows_of(way, k), :] + rrecv[way, came].astype(F32)).astype(BF16)
             rs_copy(way, pos).start()
 
-    pair_product(3)
+    pair_product(jnp.int32(3))
     for k in range(4):
         if k % 2 == 0:
             send_fresh(k)

time: 161 us -> 136 us (0.84)
  Pallas kernels: 155 us -> 131 us
    pallas_call x1, Pallas kernels: 155 us -> 131 us  [on_device(): pl.pallas_call(functools.partial(kernel, nsec), out_shape=(jax.ShapeDtype...]
where the time goes in v2:
time: 136 us
  Pallas kernels  131 us (96%)
  local copies, waits for them, and re-layouts  4.37 us (3%)
    pallas_call x1, Pallas kernels, on_device(): pl.pallas_call(functools.partial(kernel, nsec), out_shape=(jax.ShapeDtype...  131 us
    unnamed x5, local copies, waits for them, and re-layouts  4.37 us

profile of v2, /device:TPU:2, one launch (start us, length us, event | category | flops | bytes accessed | tf_op | source)
XLA Modules:
  0.0 135.6 jit_solution(9535143849780871538)
XLA Ops:
  0.6 130.6 %shard_map.112 = (bf16[128,2048]{1,0:T(8,128)(2,1)}, bf16[128,2048]{1,0:T(8,128)(2,1)}, f32[1,2048]{1,0:T(1,128)}) custom-call(bf16[128,2048]{1,0:T(8,128)(2,1)} %bitcast.10, bf16[128,2048]{1,0:T(8,128)(2,1)} %bitcast.11, bf16[128,2048]{1,0:T(8,128)(2,1)} %bitcast.12, bf16[3,2048,128]{2,1,0:T(8,128)(2,1)} %bitcast.8, bf16[128,2048]{1,0:T(8,128)(2,1)} %bitcast.13, ...), custom_call_target="tpu_custom_call" | custom-call | tf_op jit(solution)/shard_map/pallas_call | solution.py:631
  131.2 0.0 copy-start
  131.2 1.9 %copy.15 = bf16[1,128,2048]{2,1,0:T(8,128)(2,1)} copy(bf16[1,128,2048]{2,1,0:T(8,128)(2,1)} %bitcast.15) | data formatting | bytes 1048576
  133.1 1.9 %copy.16 = bf16[1,128,2048]{2,1,0:T(8,128)(2,1)} copy(bf16[1,128,2048]{2,1,0:T(8,128)(2,1)} %bitcast.14) | data formatting | bytes 1048576
  135.0 0.0 copy-done
  135.0 0.6 copy.17
Async XLA Ops:
  131.2 3.8 %copy-start = (f32[1,2048]{1,0:T(1,128)S(1)}, f32[1,2048]{1,0:T(1,128)}, u32[]{:S(2)}) copy-start(f32[1,2048]{1,0:T(1,128)} %get-tuple-element.14) | copy-start | bytes 24580

commit v3 on v2

--- a/solution.py
+++ b/solution.py
@@ -42,9 +42,8 @@
     wq_ref,
     gate_ref,
     scale_ref,
-    gain_ref,
     next_ref,
-    down_ref,
+    ig_ref,
     gg_ref,
     go_v,
     bi_v,
@@ -71,7 +70,7 @@
     xhat,
     rstd_v,
     hand,
-    down_v,
+    ig_v,
     gslots,
     ld_sem,
     ag_s,
@@ -88,7 +87,7 @@
     rs_r,
     nx_s,
     nx_r,
-    dn_sem,
+    ig_sem,
     gg_s,
     gg_r,
 ):
@@ -170,7 +169,6 @@
         for way in (0, 1):
             ag_in(way, pos).wait_recv()
             ag_out(way, pos + 2).start()
-        wq_copy(pos).start()
 
     wo_copy = pltpu.make_async_remote_copy(
         src_ref=wo_ref,
@@ -183,8 +181,8 @@
     wo_copy.start()
 
     def wq_copy(i):
-        which = lax.div(i, 2)
-        rows = pl.ds(pl.multiple_of(lax.rem(i, 2) * 64, 64), 64)
+        which = lax.div(i, 4)
+        rows = pl.ds(pl.multiple_of(lax.rem(i, 4) * 32, 32), 32)
         return pltpu.make_async_remote_copy(
             src_ref=wq_ref.at[which, rows],
             dst_ref=wcat.at[3 + which, rows],
@@ -267,6 +265,10 @@
         @pl.when(lax.rem(b, 3) == 2)
         def _():
             forward(lax.div(b, 3))
+
+        @pl.when(b > 3)
+        def _():
+            wq_copy(b - 4).start()
 
     def g_copy(d, two):
         if two:
@@ -309,47 +311,65 @@
     loads[2].wait()
     wo_copy.wait_recv()
 
-    def single(d):
-        res = mul_t(gath[zmod(z + d)], w2[...]).astype(BF16)
-        blk = 0 if d == 0 else 7
-        gsend[d, pl.ds(0, SH)] = res[:, HD:]
-        g_copy(d, False).start()
-        gblk[blk, pl.ds(0, SH)] = res[:, :HD]
-        g_copy(d, False).wait_recv()
-        backward_block(jnp.int32(blk))
-
-    single(0)
-
-    def pair(d):
-        both = jnp.concatenate([gath[zmod(z + d)], gath[zmod(z - d)]], axis=0)
-        res = mul_t(both, w2[...]).astype(BF16)
-        gsend[d] = res[:, HD:]
-        g_copy(d, True).start()
-        gblk[2 * d - 1] = res[:, :HD]
-        backward_block(2 * d - 1)
-        g_copy(d, True).wait_recv()
-        backward_block(2 * d)
-
-    forward(jnp.int32(2))
-
-    @pl.loop(1, 4)
-    def _(d):
-        pair(d)
-
-        @pl.when(d < 3)
-        def _():
-            forward(d + 2)
-
-        @pl.when(d > 1)
-        def _():
-            for way in (0, 1):
-                ag_in(way, d + 3).wait_recv()
-
-        @pl.when(d == 2)
-        def _():
-            wq_copy(jnp.int32(5)).start()
-
-    single(4)
+    def attn_grad(d):
+        two = 0 < d < 4
+        if two:
+            tokens = jnp.concatenate([gath[zmod(z + d)], gath[zmod(z - d)]], axis=0)
+        else:
+            tokens = gath[zmod(z + d)]
+        count = 2 * SH if two else SH
+        res = mul_t(tokens, w2[...]).astype(BF16)
+        gsend[d, pl.ds(0, count)] = res[:, HD:]
+        g_copy(d, two).start()
+        blk = 2 * d - 1 if d else 0
+        gblk[blk, pl.ds(0, count)] = res[:, :HD]
+
+    def arrived(pos):
+        for way in (0, 1):
+            ag_in(way, jnp.int32(pos)).wait_recv()
+
+    attn_grad(0)
+    attn_grad(1)
+
+    @pl.loop(0, 8)
+    def _(j):
+        @pl.when(j == 1)
+        def _():
+            g_copy(0, False).wait_recv()
+
+        @pl.when(j == 2)
+        def _():
+            forward(jnp.int32(2))
+            g_copy(1, True).wait_recv()
+
+        @pl.when(j == 3)
+        def _():
+            forward(jnp.int32(3))
+            attn_grad(2)
+
+        @pl.when(j == 4)
+        def _():
+            forward(jnp.int32(4))
+            g_copy(2, True).wait_recv()
+
+        @pl.when(j == 5)
+        def _():
+            arrived(5)
+            attn_grad(3)
+
+        @pl.when(j == 6)
+        def _():
+            arrived(6)
+            attn_grad(4)
+            g_copy(3, True).wait_recv()
+
+        @pl.when(j == 7)
+        def _():
+            g_copy(4, False).wait_recv()
+
+        wq_copy(4 + j).start()
+        first = 1 - lax.div(j + 6, 8)
+        backward_block(j + first * (1 - 2 * j))
 
     def x_copy(zz):
         return pltpu.make_async_remote_copy(
@@ -389,7 +409,7 @@
 
     loads[3].wait()
 
-    @pl.loop(0, 6)
+    @pl.loop(0, 12)
     def _(i):
         wq_copy(i).wait_recv()
 
@@ -489,9 +509,7 @@
     x_copy(z).wait_recv()
     product(shard_x(z), SH)
 
-    last = jnp.where(sec == nsec - 1, 1.0, 0.0).astype(F32)
     one_scale = 1.0 + scale_ref[...]
-    down_gain = gain_ref[...] + last
 
     def next_copy(q):
         rows = pl.ds(pl.multiple_of(q * QR, QR), QR)
@@ -504,9 +522,9 @@
             device_id_type=MESH,
         )
 
-    def down_copy(q):
+    def ig_copy(q):
         rows = pl.ds(pl.multiple_of(q * QR, QR), QR)
-        return pltpu.make_async_copy(down_v.at[rows], down_ref.at[rows], dn_sem.at[q])
+        return pltpu.make_async_copy(ig_v.at[rows], ig_ref.at[rows], ig_sem.at[q])
 
     def finish(q, plus_pos, minus_pos):
         rows = pl.ds(pl.multiple_of(q * QR, QR), QR)
@@ -524,8 +542,8 @@
             def _():
                 next_copy(q).start()
 
-        down_v[rows, :] = (down_gain * ig).astype(BF16)
-        down_copy(q).start()
+        ig_v[rows, :] = ig
+        ig_copy(q).start()
         return jnp.sum(ig * sk_v[rows, :].astype(F32), axis=0, keepdims=True)
 
     gain_sum = jnp.zeros((1, D), F32)
@@ -568,15 +586,6 @@
         for way in (0, 1):
             ag_out(way, pos).wait_send()
 
-    if nsec > 1:
-
-        @pl.when(sec == 0)
-        def _():
-            gath[0] = jnp.zeros((SH, D), BF16)
-            zero = pltpu.make_async_copy(gath.at[0], next_ref, nx_r.at[0])
-            zero.start()
-            zero.wait()
-
     @pl.loop(1, 2 * NZ)
     def _(off):
         gain_in(off).wait_recv()
@@ -585,7 +594,7 @@
 
     wo_copy.wait_send()
 
-    @pl.loop(0, 6)
+    @pl.loop(0, 12)
     def _(i):
         wq_copy(i).wait_send()
 
@@ -603,7 +612,7 @@
 
     @pl.loop(0, 4)
     def _(q):
-        down_copy(q).wait()
+        ig_copy(q).wait()
 
     @pl.loop(1, 2 * NZ)
     def _(off):
@@ -628,14 +637,14 @@
     any_spec = pl.BlockSpec(memory_space=pl.ANY)
     vmem_spec = pl.BlockSpec(memory_space=pltpu.VMEM)
     dma = pltpu.SemaphoreType.DMA
-    nxt, down, gg = pl.pallas_call(
+    nxt, ig, gg = pl.pallas_call(
         functools.partial(kernel, nsec),
         out_shape=(
             jax.ShapeDtypeStruct((SH, D), BF16),
-            jax.ShapeDtypeStruct((SH, D), BF16),
+            jax.ShapeDtypeStruct((SH, D), F32),
             jax.ShapeDtypeStruct((1, D), F32),
         ),
-        in_specs=[any_spec] * 6 + [vmem_spec] * 3,
+        in_specs=[any_spec] * 6 + [vmem_spec] * 2,
         out_specs=(any_spec, any_spec, vmem_spec),
         scratch_shapes=[
             pltpu.VMEM((SH, D), BF16),
@@ -663,15 +672,15 @@
             pltpu.VMEM((SH, D), F32),
             pltpu.VMEM((SH, HD), F32),
             pltpu.VMEM((SH, D), BF16),
-            pltpu.VMEM((SH, D), BF16),
+            pltpu.VMEM((SH, D), F32),
             pltpu.VMEM((2 * NZ, 1, D), F32),
             dma((6,)),
             dma((2, 7)),
             dma((2, 7)),
             dma,
             dma,
-            dma((6,)),
-            dma((6,)),
+            dma((12,)),
+            dma((12,)),
             dma((5,)),
             dma((5,)),
             dma((NZ,)),
@@ -687,7 +696,11 @@
         compiler_params=pltpu.CompilerParams(
             collective_id=0, has_side_effects=True, vmem_limit_bytes=56 * 2**20
         ),
-    )(go[0], bi[0], sk[0], qkv[0], wo[0], wq[0], gate, scale, gain)
+    )(go[0], bi[0], sk[0], qkv[0], wo[0], wq[0], gate, scale)
+    sec = lax.axis_index("section")
+    nxt = jnp.where(sec == 0, jnp.zeros_like(nxt), nxt)
+    last = jnp.where(sec == nsec - 1, 1.0, 0.0).astype(F32)
+    down = ((gain + last) * ig).astype(BF16)
     return nxt[None], down[None], gg
 
 

time: 136 us -> 120 us (0.88)
  Pallas kernels: 131 us -> 115 us
  local copies, waits for them, and re-layouts: 4.37 us -> 0.61 us
  other arithmetic: 0 us -> 2.85 us
    pallas_call x1, Pallas kernels: 131 us -> 115 us  [on_device(): pl.pallas_call(functools.partial(kernel, nsec), out_shape=(jax.ShapeDtype...]
    unnamed x5 -> x7, local copies, waits for them, and re-layouts: 4.37 us -> 0.61 us
    broadcast_in_dim x0 -> x2, other arithmetic: none -> 2.84 us  [on_device(): return (nxt[None], down[None], gg)]
where the time goes in v3:
time: 120 us; the launch traced here: 119 us
  Pallas kernels  115 us (96%)
  other arithmetic  2.85 us (2%)
    pallas_call x1, Pallas kernels, on_device(): pl.pallas_call(functools.partial(kernel, nsec), out_shape=(jax.ShapeDtype...  115 us
    broadcast_in_dim x2, other arithmetic, on_device(): return (nxt[None], down[None], gg)  2.84 us

profile of v3, /device:TPU:2, one launch (start us, length us, event | category | flops | bytes accessed | tf_op | source)
XLA Modules:
  0.0 118.7 jit_solution(14247231535662365551)
XLA Ops:
  0.6 0.0 copy-start.1
  0.6 114.6 %shard_map.112 = (bf16[128,2048]{1,0:T(8,128)(2,1)}, f32[128,2048]{1,0:T(8,128)}, f32[1,2048]{1,0:T(1,128)}) custom-call(bf16[128,2048]{1,0:T(8,128)(2,1)} %bitcast.13, bf16[128,2048]{1,0:T(8,128)(2,1)} %bitcast.14, bf16[128,2048]{1,0:T(8,128)(2,1)} %bitcast.15, bf16[3,2048,128]{2,1,0:T(8,128)(2,1)} %bitcast.11, bf16[128,2048]{1,0:T(8,128)(2,1)} %bitcast.16, ...), custom_call_target="tpu_custom_call" | custom-call | tf_op jit(solution)/shard_map/pallas_call | solution.py:640
  115.2 0.0 copy-start
  115.3 0.0 copy-start.2
  115.3 2.0 %select_bitcast_fusion = bf16[1,128,2048]{2,1,0:T(8,128)(2,1)} fusion(bf16[128,2048]{1,0:T(8,128)(2,1)} %get-tuple-element.6, pred[]{:T(512)S(6)} %eq.6), kind=kLoop, calls=%fused_computation.2 | loop fusion | flops 262144 | bytes 1048577 | tf_op jit(solution)/shard_map/broadcast_in_dim | solution.py:704
  117.2 0.0 copy-done.1
  117.2 0.0 copy-done
  117.3 0.9 fusion
  118.1 0.0 copy-done.2
  118.1 0.6 copy.13
  (1 shorter events, 0.0 us)
Async XLA Ops:
  0.6 116.6 %copy-start.1 = (f32[1,2048]{1,0:T(1,128)S(1)}, f32[1,2048]{1,0:T(1,128)}, u32[]{:S(2)}) copy-start(f32[1,2048]{1,0:T(1,128)} %param.17) | copy-start | bytes 24580
  115.2 2.0 %copy-start = (f32[128,2048]{1,0:T(8,128)S(1)}, f32[128,2048]{1,0:T(8,128)}, u32[]{:S(2)}) copy-start(f32[128,2048]{1,0:T(8,128)} %get-tuple-element.7) | copy-start | bytes 3145732
  115.3 2.9 %copy-start.2 = (f32[1,2048]{1,0:T(1,128)S(1)}, f32[1,2048]{1,0:T(1,128)}, u32[]{:S(2)}) copy-start(f32[1,2048]{1,0:T(1,128)} %get-tuple-element.14) | copy-start | bytes 24580

commit v4 on v3

--- a/solution.py
+++ b/solution.py
@@ -118,8 +118,7 @@
             ]
         )
     ]
-    for copy in loads:
-        copy.start()
+    loads[0].start()
 
     barrier = pltpu.get_barrier_semaphore()
 
@@ -138,6 +137,8 @@
         greeted += 2
 
     loads[0].wait()
+    for copy in loads[1:]:
+        copy.start()
     gath[z] = (go_v[...].astype(F32) * gate_ref[...]).astype(BF16)
     pl.semaphore_wait(barrier, greeted)
 
@@ -266,9 +267,9 @@
         def _():
             forward(lax.div(b, 3))
 
-        @pl.when(b > 3)
-        def _():
-            wq_copy(b - 4).start()
+        @pl.when(b > 2)
+        def _():
+            wq_copy(b - 3).start()
 
     def g_copy(d, two):
         if two:
@@ -367,7 +368,14 @@
         def _():
             g_copy(4, False).wait_recv()
 
-        wq_copy(4 + j).start()
+        @pl.when(j < 6)
+        def _():
+            wq_copy(5 + j).start()
+
+        @pl.when(j == 3)
+        def _():
+            wq_copy(jnp.int32(11)).start()
+
         first = 1 - lax.div(j + 6, 8)
         backward_block(j + first * (1 - 2 * j))
 

time: 120 us -> 121 us (level); the launches traced: 119 us -> 121 us
  Pallas kernels: 115 us -> 117 us
    pallas_call x1, Pallas kernels: 115 us -> 117 us  [on_device(): pl.pallas_call(functools.partial(kernel, nsec), out_shape=(jax.ShapeDtype...]
where the time goes in v4:
time: 121 us
  Pallas kernels  117 us (97%)
  other arithmetic  2.85 us (2%)
    pallas_call x1, Pallas kernels, on_device(): pl.pallas_call(functools.partial(kernel, nsec), out_shape=(jax.ShapeDtype...  117 us
    broadcast_in_dim x2, other arithmetic, on_device(): return (nxt[None], down[None], gg)  2.84 us

profile of v4, /device:TPU:2, one launch (start us, length us, event | category | flops | bytes accessed | tf_op | source)
XLA Modules:
  0.0 121.1 jit_solution(3425964309760756071)
XLA Ops:
  0.6 0.0 copy-start.1
  0.6 117.0 %shard_map.112 = (bf16[128,2048]{1,0:T(8,128)(2,1)}, f32[128,2048]{1,0:T(8,128)}, f32[1,2048]{1,0:T(1,128)}) custom-call(bf16[128,2048]{1,0:T(8,128)(2,1)} %bitcast.13, bf16[128,2048]{1,0:T(8,128)(2,1)} %bitcast.14, bf16[128,2048]{1,0:T(8,128)(2,1)} %bitcast.15, bf16[3,2048,128]{2,1,0:T(8,128)(2,1)} %bitcast.11, bf16[128,2048]{1,0:T(8,128)(2,1)} %bitcast.16, ...), custom_call_target="tpu_custom_call" | custom-call | tf_op jit(solution)/shard_map/pallas_call | solution.py:648
  117.6 0.0 copy-start
  117.7 0.0 copy-start.2
  117.7 2.0 %select_bitcast_fusion = bf16[1,128,2048]{2,1,0:T(8,128)(2,1)} fusion(bf16[128,2048]{1,0:T(8,128)(2,1)} %get-tuple-element.6, pred[]{:T(512)S(6)} %eq.6), kind=kLoop, calls=%fused_computation.2 | loop fusion | flops 262144 | bytes 1048577 | tf_op jit(solution)/shard_map/broadcast_in_dim | solution.py:712
  119.6 0.0 copy-done.1
  119.6 0.0 copy-done
  119.7 0.9 fusion
  120.5 0.0 copy-done.2
  120.5 0.6 copy.13
  (1 shorter events, 0.0 us)
Async XLA Ops:
  0.6 119.0 %copy-start.1 = (f32[1,2048]{1,0:T(1,128)S(1)}, f32[1,2048]{1,0:T(1,128)}, u32[]{:S(2)}) copy-start(f32[1,2048]{1,0:T(1,128)} %param.17) | copy-start | bytes 24580
  117.6 2.0 %copy-start = (f32[128,2048]{1,0:T(8,128)S(1)}, f32[128,2048]{1,0:T(8,128)}, u32[]{:S(2)}) copy-start(f32[128,2048]{1,0:T(8,128)} %get-tuple-element.7) | copy-start | bytes 3145732
  117.7 2.9 %copy-start.2 = (f32[1,2048]{1,0:T(1,128)S(1)}, f32[1,2048]{1,0:T(1,128)}, u32[]{:S(2)}) copy-start(f32[1,2048]{1,0:T(1,128)} %get-tuple-element.14) | copy-start | bytes 24580

commit v5 on v3

--- a/solution.py
+++ b/solution.py
@@ -262,9 +262,9 @@
     def _(b):
         softmax_block(b)
 
-        @pl.when(lax.rem(b, 3) == 2)
-        def _():
-            forward(lax.div(b, 3))
+        @pl.when(jnp.logical_and(lax.rem(b, 3) == 0, b > 0))
+        def _():
+            forward(lax.div(b, 3) - 1)
 
         @pl.when(b > 3)
         def _():

time: 120 us -> 120 us (level)
  no operation moved by 1% of the time
where the time goes in v5:
time: 120 us; the launch traced here: 119 us
  Pallas kernels  115 us (96%)
  other arithmetic  2.85 us (2%)
    pallas_call x1, Pallas kernels, on_device(): pl.pallas_call(functools.partial(kernel, nsec), out_shape=(jax.ShapeDtype...  115 us
    broadcast_in_dim x2, other arithmetic, on_device(): return (nxt[None], down[None], gg)  2.84 us

profile of v5, /device:TPU:2, one launch (start us, length us, event | category | flops | bytes accessed | tf_op | source)
XLA Modules:
  0.0 119.3 jit_solution(11971798508215285914)
XLA Ops:
  0.6 0.0 copy-start.1
  0.6 115.2 %shard_map.112 = (bf16[128,2048]{1,0:T(8,128)(2,1)}, f32[128,2048]{1,0:T(8,128)}, f32[1,2048]{1,0:T(1,128)}) custom-call(bf16[128,2048]{1,0:T(8,128)(2,1)} %bitcast.13, bf16[128,2048]{1,0:T(8,128)(2,1)} %bitcast.14, bf16[128,2048]{1,0:T(8,128)(2,1)} %bitcast.15, bf16[3,2048,128]{2,1,0:T(8,128)(2,1)} %bitcast.11, bf16[128,2048]{1,0:T(8,128)(2,1)} %bitcast.16, ...), custom_call_target="tpu_custom_call" | custom-call | tf_op jit(solution)/shard_map/pallas_call | solution.py:640
  115.8 0.0 copy-start
  115.9 0.0 copy-start.2
  115.9 2.0 %select_bitcast_fusion = bf16[1,128,2048]{2,1,0:T(8,128)(2,1)} fusion(bf16[128,2048]{1,0:T(8,128)(2,1)} %get-tuple-element.6, pred[]{:T(512)S(6)} %eq.6), kind=kLoop, calls=%fused_computation.2 | loop fusion | flops 262144 | bytes 1048577 | tf_op jit(solution)/shard_map/broadcast_in_dim | solution.py:704
  117.8 0.0 copy-done.1
  117.8 0.0 copy-done
  117.9 0.9 fusion
  118.7 0.0 copy-done.2
  118.7 0.6 copy.13
  (1 shorter events, 0.0 us)
Async XLA Ops:
  0.6 117.2 %copy-start.1 = (f32[1,2048]{1,0:T(1,128)S(1)}, f32[1,2048]{1,0:T(1,128)}, u32[]{:S(2)}) copy-start(f32[1,2048]{1,0:T(1,128)} %param.17) | copy-start | bytes 24580
  115.8 2.0 %copy-start = (f32[128,2048]{1,0:T(8,128)S(1)}, f32[128,2048]{1,0:T(8,128)}, u32[]{:S(2)}) copy-start(f32[128,2048]{1,0:T(8,128)} %get-tuple-element.7) | copy-start | bytes 3145732
  115.9 2.9 %copy-start.2 = (f32[1,2048]{1,0:T(1,128)S(1)}, f32[1,2048]{1,0:T(1,128)}, u32[]{:S(2)}) copy-start(f32[1,2048]{1,0:T(1,128)} %get-tuple-element.14) | copy-start | bytes 24580

commit v6 on v5

--- a/solution.py
+++ b/solution.py
@@ -328,6 +328,20 @@
         for way in (0, 1):
             ag_in(way, jnp.int32(pos)).wait_recv()
 
+    def layer_norm():
+        loads[4].wait()
+        loads[5].wait()
+
+        @pl.loop(0, SH // QR)
+        def _(i):
+            rows = pl.ds(pl.multiple_of(i * QR, QR), QR)
+            xv = bi_v[rows, :].astype(F32)
+            centered = xv - jnp.mean(xv, axis=-1, keepdims=True)
+            var = jnp.mean(centered * centered, axis=-1, keepdims=True)
+            rstd = 1.0 / jnp.sqrt(var + EPS)
+            xhat[rows, :] = centered * rstd
+            rstd_v[rows, :] = jnp.broadcast_to(rstd, (QR, HD))
+
     attn_grad(0)
     attn_grad(1)
 
@@ -354,6 +368,7 @@
 
         @pl.when(j == 5)
         def _():
+            layer_norm()
             arrived(5)
             attn_grad(3)
 
@@ -446,19 +461,6 @@
         for way in (0, 1):
             rsend[way, k] = ybuf[pl.ds((2 * way + k) * QR, QR), :].astype(BF16)
             rs_copy(way, k).start()
-
-    loads[4].wait()
-    loads[5].wait()
-
-    @pl.loop(0, SH // QR)
-    def _(i):
-        rows = pl.ds(pl.multiple_of(i * QR, QR), QR)
-        xv = bi_v[rows, :].astype(F32)
-        centered = xv - jnp.mean(xv, axis=-1, keepdims=True)
-        var = jnp.mean(centered * centered, axis=-1, keepdims=True)
-        rstd = 1.0 / jnp.sqrt(var + EPS)
-        xhat[rows, :] = centered * rstd
-        rstd_v[rows, :] = jnp.broadcast_to(rstd, (QR, HD))
 
     def pair_product(d):
         plus, minus = zmod(z + d), zmod(z - d)

time: 120 us -> 120 us (level)
  no operation moved by 1% of the time
where the time goes in v6:
time: 120 us; the launch traced here: 119 us
  Pallas kernels  115 us (96%)
  other arithmetic  2.85 us (2%)
    pallas_call x1, Pallas kernels, on_device(): pl.pallas_call(functools.partial(kernel, nsec), out_shape=(jax.ShapeDtype...  115 us
    broadcast_in_dim x2, other arithmetic, on_device(): return (nxt[None], down[None], gg)  2.84 us

profile of v6, /device:TPU:2, one launch (start us, length us, event | category | flops | bytes accessed | tf_op | source)
XLA Modules:
  0.0 119.3 jit_solution(1754228354156540668)
XLA Ops:
  0.6 0.0 copy-start.1
  0.6 115.2 %shard_map.112 = (bf16[128,2048]{1,0:T(8,128)(2,1)}, f32[128,2048]{1,0:T(8,128)}, f32[1,2048]{1,0:T(1,128)}) custom-call(bf16[128,2048]{1,0:T(8,128)(2,1)} %bitcast.13, bf16[128,2048]{1,0:T(8,128)(2,1)} %bitcast.14, bf16[128,2048]{1,0:T(8,128)(2,1)} %bitcast.15, bf16[3,2048,128]{2,1,0:T(8,128)(2,1)} %bitcast.11, bf16[128,2048]{1,0:T(8,128)(2,1)} %bitcast.16, ...), custom_call_target="tpu_custom_call" | custom-call | tf_op jit(solution)/shard_map/pallas_call | solution.py:642
  115.8 0.0 copy-start
  115.9 0.0 copy-start.2
  115.9 2.0 %select_bitcast_fusion = bf16[1,128,2048]{2,1,0:T(8,128)(2,1)} fusion(bf16[128,2048]{1,0:T(8,128)(2,1)} %get-tuple-element.6, pred[]{:T(512)S(6)} %eq.6), kind=kLoop, calls=%fused_computation.2 | loop fusion | flops 262144 | bytes 1048577 | tf_op jit(solution)/shard_map/broadcast_in_dim | solution.py:706
  117.8 0.0 copy-done.1
  117.8 0.0 copy-done
  117.9 0.9 fusion
  118.7 0.0 copy-done.2
  118.7 0.6 copy.13
  (1 shorter events, 0.0 us)
Async XLA Ops:
  0.6 117.2 %copy-start.1 = (f32[1,2048]{1,0:T(1,128)S(1)}, f32[1,2048]{1,0:T(1,128)}, u32[]{:S(2)}) copy-start(f32[1,2048]{1,0:T(1,128)} %param.17) | copy-start | bytes 24580
  115.8 2.0 %copy-start = (f32[128,2048]{1,0:T(8,128)S(1)}, f32[128,2048]{1,0:T(8,128)}, u32[]{:S(2)}) copy-start(f32[128,2048]{1,0:T(8,128)} %get-tuple-element.7) | copy-start | bytes 3145732
  115.9 2.9 %copy-start.2 = (f32[1,2048]{1,0:T(1,128)S(1)}, f32[1,2048]{1,0:T(1,128)}, u32[]{:S(2)}) copy-start(f32[1,2048]{1,0:T(1,128)} %get-tuple-element.14) | copy-start | bytes 24580
